TPU v7x, 32 devices: a whole 2x2x4 slice. The times are simulated.
32 devices in a mesh: groups: 2 (over y), particle: 4 (over z), head: 4 (over x, core).
Axes of the slice: x: 2, y: 2, z: 4, core: 2. Of those that a mesh axis runs over, the one named last changes fastest.
Arguments:
- tokens: int32 [64, 8], P(('groups', 'particle')), parts along dimension 0, may hold values from 0 to 64127
- ancestors: int32 [64], P(('groups', 'particle')), parts along dimension 0, may hold values from 0 to 31, as said below
- embedding: bfloat16 [64128, 4096], P('particle', 'head'), may hold values from -6 to 6
- norm_gain: bfloat16 [4096], replicated, may hold values from 0.099609375 to 1.8984375
- w_query: bfloat16 [4096, 4096], P(None, 'head'), may hold values from -0.09375 to 0.09375
- w_key: bfloat16 [4096, 1024], P(None, 'head'), may hold values from -0.09375 to 0.09375
- w_value: bfloat16 [4096, 1024], P(None, 'head'), may hold values from -0.5 to 0.5
- key_cache: bfloat16 [64, 8, 256, 128], P(('groups', 'particle'), 'head'), parts along dimension 0, may hold values from -200 to 200
- value_cache: bfloat16 [64, 8, 256, 128], P(('groups', 'particle'), 'head'), parts along dimension 0, may hold values from -6 to 6
Outputs:
- block_output: bfloat16 [64, 8, 4096], P(('groups', 'particle'), None, 'head'), parts along dimension 0
There are 2 independent parts, one for each index of `groups`. A program takes and returns all parts, laid end to end along the dimension named above; an argument that names none is the same for every part. Nothing has to cross between parts.
Inputs may be any that keep to these rules, and one draw needn't show every extreme that they name: ancestors never fall from one particle to the next; particle 0 descends from 0 and particle 32 - 1 from 31.
All inputs are finite; a program needn't handle non-finite values.
Results may differ from a plain program's by a relative error of at most 0.011.
Values may be sent and summed in bfloat16 or wider, within the bound.
A program may use at most 128 MiB of HBM per device.

v0:
```python
import math

import jax
import jax.numpy as jnp
from jax import lax
from jax.sharding import PartitionSpec as P


def angles(step_count, head_size, first_position):
    half_size = head_size // 2
    freqs = 500000.0 ** (-(2.0 * jnp.arange(half_size, dtype=jnp.float32)) / head_size)
    positions = (first_position + jnp.arange(step_count)).astype(jnp.float32)
    phase = positions[:, None] * freqs[None, :]
    return (jnp.cos(phase), jnp.sin(phase))


def rotate(values, cosine_table, sine_table):
    half_size = values.shape[-1] // 2
    front_half = values[..., :half_size]
    back_half = values[..., half_size:]
    return jnp.concatenate(
        [
            front_half * cosine_table - back_half * sine_table,
            back_half * cosine_table + front_half * sine_table,
        ],
        axis=-1,
    )


def per_device(
    tokens, ancestors, embedding, norm_gain, w_query, w_key, w_value, key_cache, value_cache
):
    particles, step_count = tokens.shape
    head_size = key_cache.shape[3]
    local_kv = key_cache.shape[1]
    context = key_cache.shape[2]
    local_heads = w_query.shape[1] // head_size
    group_size = local_heads // local_kv
    vocab_rows = embedding.shape[0]
    my_index = lax.axis_index("particle")
    score_scale = 1.0 / math.sqrt(head_size)
    all_tokens, all_parents = (
        lax.all_gather(tokens, "particle", axis=0, tiled=True),
        lax.all_gather(ancestors, "particle", axis=0, tiled=True),
    )
    flat_ids = all_tokens.reshape(-1) - my_index * vocab_rows
    vocab_iota = jnp.arange(vocab_rows, dtype=jnp.int32)
    one_hot = (flat_ids[:, None] == vocab_iota[None, :]).astype(jnp.bfloat16)
    own_rows = lax.psum_scatter(
        jnp.dot(one_hot, embedding, preferred_element_type=jnp.float32).astype(jnp.bfloat16),
        "particle",
        scatter_dimension=0,
        tiled=True,
    )
    embedded = lax.all_gather(own_rows, "head", axis=1, tiled=True).astype(jnp.float32)
    mean_square = jnp.mean(embedded * embedded, axis=-1, keepdims=True)
    normed = (embedded * lax.rsqrt(mean_square + 1e-05) * norm_gain.astype(jnp.float32)).astype(
        jnp.bfloat16
    )
    cosine_table, sine_table = angles(step_count, head_size, context)
    queries = jnp.dot(normed, w_query, preferred_element_type=jnp.float32).reshape(
        particles, step_count, local_kv, group_size, head_size
    )
    queries = rotate(
        queries, cosine_table[None, :, None, None, :], sine_table[None, :, None, None, :]
    ).astype(jnp.bfloat16)
    new_keys = jnp.dot(normed, w_key, preferred_element_type=jnp.float32).reshape(
        particles, step_count, local_kv, head_size
    )
    new_keys = rotate(
        new_keys, cosine_table[None, :, None, :], sine_table[None, :, None, :]
    ).astype(jnp.bfloat16)
    new_values = (
        jnp.dot(normed, w_value, preferred_element_type=jnp.float32)
        .reshape(particles, step_count, local_kv, head_size)
        .astype(jnp.bfloat16)
    )
    causal = jnp.arange(step_count)[:, None] >= jnp.arange(step_count)[None, :]
    own_scores = (
        jnp.einsum("pskgd,prkd->pskgr", queries, new_keys, preferred_element_type=jnp.float32)
        * score_scale
    )
    own_scores = jnp.where(causal[None, :, None, None, :], own_scores, -jnp.inf)
    own_top = jnp.max(own_scores, axis=-1)
    own_weights = jnp.exp(own_scores - own_top[..., None])
    own_total = jnp.sum(own_weights, axis=-1)
    own_accum = jnp.einsum("pskgr,prkd->pskgd", own_weights, new_values.astype(jnp.float32))
    every_query = lax.all_gather(queries, "particle", axis=0, tiled=True)
    local_parent = all_parents - my_index * particles
    selected = local_parent[:, None] == jnp.arange(particles, dtype=jnp.int32)[None, :]
    present = jnp.any(selected, axis=-1)
    chosen = selected.astype(jnp.bfloat16)
    child_keys = jnp.einsum(
        "cj,jktd->cktd", chosen, key_cache, preferred_element_type=jnp.float32
    ).astype(jnp.bfloat16)
    child_values = jnp.einsum(
        "cj,jktd->cktd", chosen, value_cache, preferred_element_type=jnp.float32
    )
    scores = (
        jnp.einsum("cskgd,cktd->cskgt", every_query, child_keys, preferred_element_type=jnp.float32)
        * score_scale
    )
    highest = jnp.max(scores, axis=-1)
    highest = jnp.where(present[:, None, None, None], highest, 0.0)
    weights = jnp.exp(scores - highest[..., None])
    weights = jnp.where(present[:, None, None, None, None], weights, 0.0)
    totals = jnp.sum(weights, axis=-1)
    accum = jnp.einsum("cskgt,cktd->cskgd", weights, child_values)
    cache_accum, cache_total, cache_top = (
        lax.psum_scatter(accum, "particle", scatter_dimension=0, tiled=True),
        lax.psum_scatter(totals, "particle", scatter_dimension=0, tiled=True),
        lax.psum_scatter(highest, "particle", scatter_dimension=0, tiled=True),
    )
    highest = jnp.maximum(cache_top, own_top)
    cache_factor = jnp.exp(cache_top - highest)
    own_factor = jnp.exp(own_top - highest)
    accum = cache_accum * cache_factor[..., None] + own_accum * own_factor[..., None]
    totals = cache_total * cache_factor + own_total * own_factor
    attended = (accum / totals[..., None]).astype(jnp.bfloat16)
    return attended.reshape(particles, step_count, local_heads * head_size)


def solution(mesh):
    in_specs = (
        P(("groups", "particle"), None),
        P(("groups", "particle")),
        P("particle", "head"),
        P(),
        P(None, "head"),
        P(None, "head"),
        P(None, "head"),
        P(("groups", "particle"), "head", None, None),
        P(("groups", "particle"), "head", None, None),
    )
    out_specs = P(("groups", "particle"), None, "head")
    return jax.shard_map(
        per_device, mesh=mesh, in_specs=in_specs, out_specs=out_specs, check_vma=False
    )
```

profile of v0, /device:TPU:0, one launch (start us, length us, event | category | flops | bytes accessed | tf_op | source)
XLA Modules:
  0.0 145.9 jit_solution(16687848579476327255)
XLA Ops:
  6.5 0.0 copy-start
  6.5 0.0 reduce-scatter.3.cloned.1.call-start
  6.5 15.1 %all_gather.13 = s32[32,8]{1,0:T(8,128)S(1)} all-gather(s32[8,8]{1,0:T(8,128)} %param.9), channel_id=1, replica_groups=mesh['groups'=2,'particle'=4,'head'=4] {'particle'}, dimensions={0}, use_global_device_ids=true | all-gather | bytes 1280 | tf_op jit(solution)/shard_map/all_gather | solution.py:43
  21.6 0.1 sub.51
  21.7 0.0 copy-start.6
  21.7 0.0 copy-start.7
  21.7 0.0 copy-start.8
  21.7 0.0 copy-start.4
  21.7 15.3 %fusion.15 = bf16[256,1024]{1,0:T(8,128)(2,1)} fusion(bf16[16032,1024]{1,0:T(8,128)(2,1)} %param.11, s32[256]{0:T(256)S(1)} %sub.51), kind=kOutput, calls=%fused_computation.17 | convolution fusion | flops 8409751552 | bytes 33358848 | tf_op jit(solution)/shard_map/dot_general | solution.py:50
  37.1 0.0 reduce-scatter.3.cloned.1.call-update
  37.1 0.0 reduce-scatter.5.cloned.1.call-start
  37.2 0.0 copy-done.6
  37.2 0.0 copy-done.7
  37.2 0.7 fusion.55
  38.6 0.0 copy-done.8
  38.6 0.2 dynamic-update-slice
  38.9 7.9 %all-reduce = s32[32]{0:T(128)S(1)} all-reduce(s32[32]{0:T(128)S(1)} %dynamic-update-slice), channel_id=1, replica_groups=mesh['groups'=2,'particle'=4,'head'=4] {'particle'}, use_global_device_ids=true, to_apply=%add | all-reduce | flops 32 | bytes 256
  46.8 0.0 copy-done.4
  46.8 0.0 copy-start.5
  46.8 3.3 %convert_bitcast_fusion = bf16[32,2,256,128,1]{3,0,2,1,4:T(8,128)(2,1)} fusion(bf16[8,2,256,128]{3,2,1,0:T(8,128)(2,1)S(1)} %copy-done.4, s32[32]{0:T(128)S(1)} %broadcast_subtract_fusion.1), kind=kOutput, calls=%fused_computation.7 | convolution fusion | flops 35651840 | bytes 5243008 | tf_op jit(solution)/shard_map/cj,jktd->cktd/dot_general | solution.py:93
  50.1 0.0 copy-done.5
  50.1 3.2 %convolution_bitcast_fusion = bf16[32,2,256,128,1]{3,0,2,1,4:T(8,128)(2,1)} fusion(bf16[8,2,256,128]{3,2,1,0:T(8,128)(2,1)S(1)} %copy-done.5, s32[32]{0:T(128)S(1)} %broadcast_subtract_fusion.1), kind=kOutput, calls=%fused_computation.8 | convolution fusion | flops 33554688 | bytes 5243008 | tf_op jit(solution)/shard_map/cj,jktd->cktd/dot_general | solution.py:96
  53.3 0.1 multiply_cosine_fusion
  53.4 6.5 %reduce-scatter.3.cloned.1.call-done = bf16[64,1024]{1,0:T(8,128)(2,1)} async-done(((bf16[256,1024]{1,0:T(8,128)(2,1)}), bf16[64,1024]{1,0:T(8,128)(2,1)}) %reduce-scatter.3.cloned.1.call-update) | async-done | bytes 131088 | tf_op jit(solution)/shard_map/reduce_scatter | solution.py:49
  59.9 7.3 %all_gather.14 = bf16[64,4096]{1,0:T(8,128)(2,1)S(1)} all-gather(bf16[64,1024]{1,0:T(8,128)(2,1)} %reduce-scatter.3.cloned.1.call-done), channel_id=1, replica_groups=mesh['groups'=2,'particle'=4,'head'=4] {'head'}, dimensions={1}, use_global_device_ids=true | all-gather | bytes 655360 | tf_op jit(solution)/shard_map/all_gather | solution.py:55
  67.2 0.2 fusion.23
  67.4 0.0 copy-start.2
  67.4 5.2 %fusion.51 = f32[64,1024]{1,0:T(8,128)S(1)} fusion(bf16[4096,1024]{1,0:T(8,128)(2,1)} %param.13, bf16[64,4096]{1,0:T(8,128)(2,1)S(1)} %all_gather.14, f32[4096]{0:T(1024)S(1)} %convert_element_type.53, f32[64]{0:T(128)S(1)} %add_rsqrt_fusion), kind=kOutput, calls=%fused_computation.72 | convolution fusion | flops 537919488 | bytes 9191680 | tf_op jit(solution)/shard_map/dot_general | solution.py:61
  72.6 0.2 subtract_convert_fusion
  72.7 0.1 pad_maximum_fusion
  72.8 16.3 %all_gather.15 = bf16[32,8,2,4,128]{4,1,3,2,0:T(8,128)(2,1)S(1)} all-gather(bf16[8,8,2,4,128]{4,1,3,2,0:T(8,128)(2,1)S(1)} %pad_maximum_fusion), channel_id=1, replica_groups=mesh['groups'=2,'particle'=4,'head'=4] {'particle'}, dimensions={0}, use_global_device_ids=true | all-gather | bytes 655360 | tf_op jit(solution)/shard_map/all_gather | solution.py:88
  89.1 0.0 copy-done.2
  89.1 0.0 copy-start.1
  89.1 4.5 %bitcast_reduce_fusion = (f32[32,8,2,4]{1,3,2,0:T(4,128)S(1)}, f32[32,2,256,8,4]{2,3,4,1,0:T(8,128)S(1)}) fusion(bf16[32,8,2,4,128]{4,1,3,2,0:T(8,128)(2,1)S(1)} %all_gather.15, bf16[32,2,256,128,1]{3,0,2,1,4:T(8,128)(2,1)S(1)} %copy-done.2), kind=kOutput, calls=%fused_computation.10 | convolution fusion | flops 135264256 | bytes 6823936 | tf_op jit(solution)/shard_map/cskgd,cktd->cskgt/dot_general | solution.py:100
  93.6 0.1 broadcast_select_fusion
  93.7 1.2 copy-done.3
  94.9 0.0 copy-done.1
  94.9 5.6 %fusion.10 = f32[32,8,2,4,128]{4,1,3,2,0:T(8,128)} fusion(f32[32,2,256,8,4]{2,3,4,1,0:T(8,128)S(1)} %get-tuple-element.19, bf16[32,2,256,128,1]{3,0,2,1,4:T(8,128)(2,1)S(1)} %copy-done.1, f32[32,8,2,4]{1,3,2,0:T(4,128)S(1)} %broadcast_select_fusion, pred[32]{0:T(512)(128)(4,1)S(1)} %fusion.39), kind=kOutput, calls=%fused_computation.14 | convolution fusion | flops 135790592 | bytes 7348256 | tf_op jit(solution)/shard_map/cskgt,cktd->cskgd/dot_general | solution.py:108
  100.5 0.0 reduce-scatter.5.cloned.1.call-update
  101.2 2.5 %fusion.8 = f32[32,8,2,4]{1,3,2,0:T(4,128)S(1)} fusion(f32[32,2,256,8,4]{2,3,4,1,0:T(8,128)} %copy-done.3, f32[32,8,2,4]{1,3,2,0:T(4,128)S(1)} %broadcast_select_fusion, pred[32]{0:T(512)(128)(4,1)S(1)} %fusion.39), kind=kLoop, calls=%fused_computation.13 | loop fusion | flops 2095104 | bytes 2113568 | tf_op jit(solution)/shard_map/reduce_sum | solution.py:107
  103.7 29.9 %all-reduce.3 = (f32[32,8,2,4]{1,3,2,0:T(4,128)S(1)}, f32[32,8,2,4]{1,3,2,0:T(4,128)S(1)}) all-reduce(f32[32,8,2,4]{1,3,2,0:T(4,128)S(1)} %broadcast_select_fusion, f32[32,8,2,4]{1,3,2,0:T(4,128)S(1)} %fusion.8), channel_id=4, replica_groups=mesh['groups'=2,'particle'=4,'head'=4] {'particle'}, use_global_device_ids=true, to_apply=%region_5.6.clone | all-reduce | flops 4096 | bytes 32768
  133.5 2.1 %convolution_bitcast_fusion.2 = f32[8,8,2,128]{3,1,2,0:T(8,128)S(1)} fusion(bf16[4096,256]{1,0:T(8,128)(2,1)} %param.14, bf16[64,4096]{1,0:T(8,128)(2,1)S(1)} %all_gather.14, f32[4096]{0:T(1024)S(1)} %convert_element_type.53, f32[64]{0:T(128)S(1)} %add_rsqrt_fusion), kind=kOutput, calls=%fused_computation.26 | convolution fusion | flops 135266304 | bytes 2703616 | tf_op jit(solution)/shard_map/dot_general | solution.py:67
  135.6 0.1 subtract_convert_fusion.1
  135.7 0.7 fusion.56
  136.5 0.1 fusion.32
  136.7 0.0 reduce-scatter.5.cloned.1.call-done
  136.7 0.0 copy-done
  136.7 2.3 %fusion.21 = bf16[8,8,2,4,128]{4,1,3,2,0:T(8,128)(2,1)} fusion(bf16[4096,256]{1,0:T(8,128)(2,1)S(1)} %copy-done, f32[8,8,2,4,128]{4,1,3,2,0:T(8,128)} %reduce-scatter.5.cloned.1.call-done, f32[8,8,2,4,8]{1,4,3,2,0:T(8,128)S(1)} %get-tuple-element.21, f32[8,8,2,4]{1,3,2,0:T(4,128)S(1)} %get-tuple-element.7, f32[8,8,2,4]{1,3,2,0:T(4,128)S(1)} %get-tuple-element.8, ...), kind=kOutput, calls=%fused_computation.25 | convolution fusion | flops 136663040 | bytes 3055872 | tf_op jit(solution)/shard_map/pskgr,prkd->pskgd/dot_general | solution.py:87
  (11 shorter events, 0.1 us)
Async XLA Ops:
  6.5 130.2 %copy-start = (bf16[4096,256]{1,0:T(8,128)(2,1)S(1)}, bf16[4096,256]{1,0:T(8,128)(2,1)}, u32[]{:S(2)}) copy-start(bf16[4096,256]{1,0:T(8,128)(2,1)} %param.15) | copy-start | bytes 6291460
  6.5 53.4 %reduce-scatter.3.cloned.1.call-start = ((), (), s32[]{:S(2)}) async-start(), calls=%async_computation.2 | async-start | bytes 655360 | tf_op jit(solution)/shard_map/reduce_scatter | solution.py:49
  21.7 15.5 %copy-start.6 = (bf16[4096]{0:T(1024)(128)(2,1)S(1)}, bf16[4096]{0:T(1024)(128)(2,1)}, u32[]{:S(2)}) copy-start(bf16[4096]{0:T(1024)(128)(2,1)} %param.12) | copy-start | bytes 24580
  21.7 15.5 %copy-start.7 = (u32[32]{0:T(128)S(1)}, u32[32]{0:T(128)}, u32[]{:S(2)}) copy-start(u32[32]{0:T(128)} %constant.36) | copy-start | bytes 388
  21.7 16.9 %copy-start.8 = (s32[8]{0:T(128)S(1)}, s32[8]{0:T(128)}, u32[]{:S(2)}) copy-start(s32[8]{0:T(128)} %param.10) | copy-start | bytes 100
  21.7 25.1 %copy-start.4 = (bf16[8,2,256,128]{3,2,1,0:T(8,128)(2,1)S(1)}, bf16[8,2,256,128]{3,2,1,0:T(8,128)(2,1)}, u32[]{:S(2)}) copy-start(bf16[8,2,256,128]{3,2,1,0:T(8,128)(2,1)} %param.16) | copy-start | bytes 3145732
  37.1 99.6 %reduce-scatter.5.cloned.1.call-start = ((), (), s32[]{:S(2)}) async-start(), calls=%async_computation.3 | async-start | bytes 1310720 | tf_op jit(solution)/shard_map/reduce_scatter | solution.py:110
  46.8 3.3 %copy-start.5 = (bf16[8,2,256,128]{3,2,1,0:T(8,128)(2,1)S(1)}, bf16[8,2,256,128]{3,2,1,0:T(8,128)(2,1)}, u32[]{:S(2)}) copy-start(bf16[8,2,256,128]{3,2,1,0:T(8,128)(2,1)} %param.17) | copy-start | bytes 3145732
  67.4 21.7 %copy-start.2 = (bf16[32,2,256,128,1]{3,0,2,1,4:T(8,128)(2,1)S(1)}, bf16[32,2,256,128,1]{3,0,2,1,4:T(8,128)(2,1)}, u32[]{:S(2)}) copy-start(bf16[32,2,256,128,1]{3,0,2,1,4:T(8,128)(2,1)} %convert_bitcast_fusion) | copy-start | bytes 12582916
  89.1 5.8 %copy-start.1 = (bf16[32,2,256,128,1]{3,0,2,1,4:T(8,128)(2,1)S(1)}, bf16[32,2,256,128,1]{3,0,2,1,4:T(8,128)(2,1)}, u32[]{:S(2)}) copy-start(bf16[32,2,256,128,1]{3,0,2,1,4:T(8,128)(2,1)} %convolution_bitcast_fusion) | copy-start | bytes 12582916
  93.6 1.3 copy-start.3
Sparse Core Ops, SparseCore 0:
  37.2 22.6 reduce-scatter.2
  100.6 31.1 reduce-scatter.4
where the time goes:
time: 146 us
  blocking collectives  76.3 us (52%)
  matrix products  42.2 us (29%)
  between operations  15 us (10%)
  waiting for transfers between devices  6.58 us (5%)
  other arithmetic  3.46 us (2%)
  local copies, waits for them, and re-layouts  2.26 us (2%)
    unnamed x2, blocking collectives  37.8 us
    all_gather x1, blocking collectives, per_device(): every_query = lax.all_gather(queries, 'particle', axis=0, tiled=True)  16.3 us
    dot_general x1, matrix products, per_device(): jnp.dot(one_hot, embedding, preferred_element_type=jnp.float32)  15.3 us
    all_gather x1, blocking collectives, per_device(): lax.all_gather(tokens, 'particle', axis=0, tiled=True)  15.1 us
    all_gather x1, blocking collectives, per_device(): lax.all_gather(own_rows, 'head', axis=1, tiled=True).astype(jnp.float32)  7.26 us
    reduce_scatter x1, waiting for transfers between devices, per_device(): lax.psum_scatter(jnp.dot(one_hot, embedding, preferred_element_type=jnp.f...  6.52 us
    dot_general x1, matrix products, per_device(): accum = jnp.einsum('cskgt,cktd->cskgd', weights, child_values)  5.56 us
    dot_general x1, matrix products, per_device(): jnp.dot(normed, w_query, preferred_element_type=jnp.float32)  5.15 us
  transfers between devices with their start and end apart: 2, of which 1 were waited for; matrix products, arithmetic and copies ran while one was open for 9% of the time, Pallas kernels for 0%

commit v1 on v0

v1 whole, which is shorter than its diff:
```python
import functools
import math

import jax
import jax.numpy as jnp
import numpy as np
from jax import lax
from jax.experimental import pallas as pl
from jax.experimental.pallas import tpu as pltpu
from jax.sharding import PartitionSpec as P

MESH = pl.DeviceIdType.MESH
VMEM_LIMIT = 48 * 1024 * 1024


def remote(src, dst, send_sem, recv_sem, **where):
    return pltpu.make_async_remote_copy(
        src_ref=src,
        dst_ref=dst,
        send_sem=send_sem,
        recv_sem=recv_sem,
        device_id=where,
        device_id_type=MESH,
    )


def ids_kernel(n, ids_ref, all_ref, send_sem, recv_sem):
    me = lax.axis_index("particle")
    peers = [lax.rem(me + r, n) for r in range(1, n)]
    barrier = pltpu.get_barrier_semaphore()
    for peer in peers:
        pl.semaphore_signal(barrier, inc=1, device_id={"particle": peer}, device_id_type=MESH)
    pl.semaphore_wait(barrier, n - 1)
    copies = [
        remote(ids_ref, all_ref.at[me], send_sem.at[r], recv_sem.at[r], particle=peer)
        for r, peer in enumerate(peers)
    ]
    for copy in copies:
        copy.start()
    all_ref[me] = ids_ref[...]
    for copy in copies:
        copy.wait()


def rows_kernel(n, particles, steps, tile, ids_ref, table_ref, out_ref, blocks, found, listed, sem):
    vocab_rows = table_ref.shape[0]
    first = lax.axis_index("particle") * vocab_rows
    per_device = particles * steps

    def look(member, count):
        owner = member // particles
        child = lax.rem(member, particles)
        for step in range(steps):
            local = ids_ref[owner, child, step] - first
            token = member * steps + step
            owned = jnp.logical_and(local >= 0, local < vocab_rows)
            listed[0, count] = token
            listed[1, count] = local

            @pl.when(owned)
            def _():
                start = pl.multiple_of((local // tile) * tile, tile)
                pltpu.make_async_copy(
                    table_ref.at[pl.ds(start, tile)], blocks.at[count], sem
                ).start()

            count = count + owned.astype(jnp.int32)
        return count

    found[...] = jnp.zeros_like(found)
    count = lax.fori_loop(0, n * particles, look, 0)

    def arrive(slot, carry):
        pltpu.make_async_copy(table_ref.at[pl.ds(0, tile)], blocks.at[slot], sem).wait()
        return carry

    lax.fori_loop(0, count, arrive, 0)

    def pick(slot, carry):
        token, local = listed[0, slot], listed[1, slot]
        row = lax.rem(local, tile)
        block = blocks[slot].astype(jnp.float32)
        here = lax.broadcasted_iota(jnp.int32, block.shape, 0) == row
        found[pl.ds(token, 1), :] = jnp.sum(jnp.where(here, block, 0.0), axis=0, keepdims=True)
        return carry

    lax.fori_loop(0, count, pick, 0)
    out_ref[...] = found[...].astype(out_ref.dtype)


def main_kernel(
    n,
    heads,
    deltas,
    widths,
    ids_ref,
    rows_ref,
    gain_ref,
    cos_ref,
    sin_ref,
    wq_hbm,
    wk_hbm,
    wv_hbm,
    kc_hbm,
    vc_hbm,
    out_ref,
    wq,
    wk,
    wv,
    kc,
    vc,
    came,
    emb,
    proj,
    query,
    new_k,
    new_v,
    q_in,
    res_out,
    lse_out,
    res_in,
    lse_in,
    own_res,
    load_sem,
    a_send,
    a_recv,
    x_send,
    x_recv,
    s_send,
    s_recv,
    q_send,
    q_recv,
    r_send,
    r_recv,
    l_send,
    l_recv,
):
    particles, kv = kc.shape[0], kc.shape[1]
    steps = cos_ref.shape[0]
    head_size = kc.shape[3]
    tokens = particles * steps
    local_heads = wq.shape[1] // head_size
    group = local_heads // kv
    rows = group * steps
    depth = rows_ref.shape[1]
    scale = 1.0 / math.sqrt(head_size)
    z = lax.axis_index("particle")
    h = lax.axis_index("head")
    cores = 2
    chips = heads // cores
    chip, core = h // cores, lax.rem(h, cores)
    sibling = chip * cores + 1 - core

    loads = [
        pltpu.make_async_copy(src, dst, load_sem.at[i])
        for i, (src, dst) in enumerate(
            ((wq_hbm, wq), (wk_hbm, wk), (wv_hbm, wv), (kc_hbm, kc), (vc_hbm, vc))
        )
    ]
    for load in loads:
        load.start()

    z_peers = [lax.rem(z + r, n) for r in range(1, n)]
    x_peers = [lax.rem(chip + r, chips) * cores + core for r in range(1, chips)]
    x_from = [lax.rem(chip - r + chips, chips) * cores + core for r in range(1, chips)]
    barrier = pltpu.get_barrier_semaphore()
    for peer in z_peers:
        pl.semaphore_signal(barrier, inc=1, device_id={"particle": peer}, device_id_type=MESH)
    for peer in x_peers + [sibling]:
        pl.semaphore_signal(barrier, inc=1, device_id={"head": peer}, device_id_type=MESH)
    pl.semaphore_wait(barrier, n - 1 + chips)

    a_copies = [
        remote(
            rows_ref.at[pl.ds(pl.multiple_of(peer * tokens, tokens), tokens)],
            came.at[r],
            a_send.at[r],
            a_recv.at[r],
            particle=peer,
        )
        for r, peer in enumerate(z_peers)
    ]
    for copy in a_copies:
        copy.start()
    total = rows_ref[pl.ds(pl.multiple_of(z * tokens, tokens), tokens), :]
    for r, copy in enumerate(a_copies):
        copy.wait_recv()
        total = total + came[r]
    emb[h] = total

    sib_own = remote(emb.at[h], emb.at[h], s_send.at[0], s_recv.at[0], head=sibling)
    x_copies = [
        remote(emb.at[h], emb.at[h], x_send.at[r], x_recv.at[r], head=peer)
        for r, peer in enumerate(x_peers)
    ]
    for copy in x_copies:
        copy.start()
    sib_own.start()
    for load in loads[:3]:
        load.wait()

    square = jnp.zeros((tokens, 1), jnp.float32)

    def contract(square, index, first):
        part = emb[index].astype(jnp.float32)
        square = square + jnp.sum(part * part, axis=1, keepdims=True)
        at = pl.ds(pl.multiple_of(index * depth, depth), depth)
        scaled = (part * gain_ref[:, at].astype(jnp.float32)).astype(jnp.bfloat16)
        column = 0
        for weight in (wq, wk, wv):
            for begin in range(0, weight.shape[1], 128 if weight.shape[1] % 256 else 256):
                width = 128 if weight.shape[1] % 256 else 256
                product = jnp.dot(
                    scaled,
                    weight[at, begin : begin + width],
                    preferred_element_type=jnp.float32,
                )
                where = slice(column, column + width)
                if first:
                    proj[:, where] = product
                else:
                    proj[:, where] += product
                column += width
        return square

    square = contract(square, h, True)
    sib_own.wait_recv()
    square = contract(square, sibling, False)
    forwards = []
    for r, (copy, source) in enumerate(zip(x_copies, x_from)):
        copy.wait_recv()
        forward = remote(
            emb.at[source], emb.at[source], s_send.at[r + 1], s_recv.at[r + 1], head=sibling
        )
        forward.start()
        forwards.append(forward)
        square = contract(square, source, False)
    for r, forward in enumerate(forwards):
        forward.wait_recv()
        source = lax.rem(chip - (r + 1) + chips, chips) * cores + 1 - core
        square = contract(square, source, False)

    norm = lax.rsqrt(square * (1.0 / (depth * heads)) + 1e-5)
    cosine, sine = cos_ref[...], sin_ref[...]

    def spin(column):
        value = proj[:, column * head_size : (column + 1) * head_size] * norm
        turned = pltpu.roll(value, head_size // 2, 1)
        shape = (particles, steps, head_size)
        return value.reshape(shape) * cosine[None] + turned.reshape(shape) * sine[None]

    for k in range(kv):
        for pair in range(0, group, 2):
            both = jnp.concatenate([spin(k * group + pair), spin(k * group + pair + 1)], axis=1)
            query[:, k, pair * steps : (pair + 2) * steps, :] = both.astype(jnp.bfloat16)

    def span(d):
        width = widths[abs(d)]
        return (0 if d < 0 else particles - width), width

    def reaches(d):
        return jnp.logical_and(z + d >= 0, z + d < n)

    def query_copy(i, d):
        begin, width = span(d)
        return remote(
            query.at[pl.ds(begin, width)],
            q_in.at[i, pl.ds(begin, width)],
            q_send.at[i],
            q_recv.at[i],
            particle=z + d,
        )

    def back_copies(i, d):
        begin, width = span(d)
        return (
            remote(
                res_out.at[i, pl.ds(begin, width)],
                res_in.at[i, pl.ds(begin, width)],
                r_send.at[i],
                r_recv.at[i],
                particle=z - d,
            ),
            remote(
                lse_out.at[i], lse_in.at[i], l_send.at[i], l_recv.at[i], particle=z - d
            ),
        )

    for i, d in enumerate(deltas):

        @pl.when(reaches(d))
        def _():
            query_copy(i, d).start()

    for k in range(kv):
        new_k[k] = spin(local_heads + k).reshape(tokens, head_size).astype(jnp.bfloat16)
        base = (local_heads + kv + k) * head_size
        new_v[k] = (proj[:, base : base + head_size] * norm).astype(jnp.bfloat16)

    own_lse = []
    for k in range(kv):
        q_rows = query[:, k].reshape(particles * rows, head_size)
        scores = lax.dot_general(
            q_rows, new_k[k], (((1,), (1,)), ((), ())), preferred_element_type=jnp.float32
        ) * scale
        at_row = lax.broadcasted_iota(jnp.int32, scores.shape, 0)
        at_key = lax.broadcasted_iota(jnp.int32, scores.shape, 1)
        seen = jnp.logical_and(
            at_row // rows == at_key // steps,
            lax.rem(at_key, steps) <= lax.rem(at_row, steps),
        )
        scores = jnp.where(seen, scores, -1e30)
        top = jnp.max(scores, axis=1, keepdims=True)
        weight = jnp.exp(scores - top)
        weight = jnp.where(seen, weight, 0.0)
        amount = jnp.sum(weight, axis=1, keepdims=True)
        summed = jnp.dot(weight.astype(jnp.bfloat16), new_v[k], preferred_element_type=jnp.float32)
        own_res[k] = summed / amount
        own_lse.append(top + jnp.log(amount))

    for load in loads[3:]:
        load.wait()

    lane = lax.broadcasted_iota(jnp.int32, (rows, 128), 1)

    def attend(i, source_query, begin, width, source):
        some = 4 if width % 4 == 0 else 1

        def some_children(block, lse):
            for offset in range(some):
                child = begin + block * some + offset
                parent = ids_ref[source, child, steps] - z * particles
                parent = jnp.minimum(jnp.maximum(parent, 0), particles - 1)
                for k in range(kv):
                    scores = lax.dot_general(
                        source_query(child, k),
                        kc[parent, k],
                        (((1,), (1,)), ((), ())),
                        preferred_element_type=jnp.float32,
                    ) * scale
                    top = jnp.max(scores, axis=1, keepdims=True)
                    weight = jnp.exp(scores - top)
                    amount = jnp.sum(weight, axis=1, keepdims=True)
                    summed = jnp.dot(
                        weight.astype(jnp.bfloat16),
                        vc[parent, k],
                        preferred_element_type=jnp.float32,
                    )
                    res_out[i, child, k] = (summed / amount).astype(jnp.bfloat16)
                    lse = jnp.where(lane == child * kv + k, top + jnp.log(amount), lse)
            return lse

        lse_out[i] = lax.fori_loop(
            0, width // some, some_children, jnp.zeros((rows, 128), jnp.float32)
        )

    own = len(deltas)
    attend(own, lambda child, k: query[child, k], 0, particles, z)
    res_in[own] = res_out[own]
    lse_in[own] = lse_out[own]

    for i, d in enumerate(deltas):

        @pl.when(reaches(-d))
        def _():
            query_copy(i, d).wait_recv()
            begin, width = span(d)
            attend(i, lambda child, k: q_in[i, child, k], begin, width, z - d)
            for copy in back_copies(i, d):
                copy.start()

    for i, d in enumerate(deltas):

        @pl.when(reaches(d))
        def _():
            for copy in back_copies(i, d):
                copy.wait_recv()

    for child in range(particles):
        owner = ids_ref[z, child, steps] // particles
        slot = jnp.int32(own)
        for i, d in enumerate(deltas):
            slot = jnp.where(owner - z == d, i, slot)
        parts = []
        lse_tile = lse_in[slot]
        for k in range(kv):
            cached = res_in[slot, child, k].astype(jnp.float32)
            cached_lse = jnp.sum(
                jnp.where(lane == child * kv + k, lse_tile, 0.0), axis=1, keepdims=True
            )
            at = slice(child * rows, (child + 1) * rows)
            mine, mine_lse = own_res[k, at, :], own_lse[k][at, :]
            top = jnp.maximum(cached_lse, mine_lse)
            cached_factor = jnp.exp(cached_lse - top)
            mine_factor = jnp.exp(mine_lse - top)
            mixed = (cached * cached_factor + mine * mine_factor) / (cached_factor + mine_factor)
            for g in range(group):
                parts.append(mixed[g * steps : (g + 1) * steps, :])
        out_ref[child] = jnp.concatenate(parts, axis=1).astype(out_ref.dtype)

    for copy in a_copies + x_copies + forwards + [sib_own]:
        copy.wait_send()
    for i, d in enumerate(deltas):

        @pl.when(reaches(d))
        def _():
            query_copy(i, d).wait_send()

        @pl.when(reaches(-d))
        def _():
            for copy in back_copies(i, d):
                copy.wait_send()


def tables(steps, head_size, first_position):
    half = head_size // 2
    freqs = 500000.0 ** (-(2.0 * np.arange(half)) / head_size)
    phase = (first_position + np.arange(steps))[:, None] * freqs[None, :]
    cosine, sine = np.cos(phase), np.sin(phase)
    return (
        np.concatenate([cosine, cosine], axis=1).astype(np.float32),
        np.concatenate([-sine, sine], axis=1).astype(np.float32),
    )


def per_device(
    n,
    heads,
    tokens,
    ancestors,
    embedding,
    norm_gain,
    w_query,
    w_key,
    w_value,
    key_cache,
    value_cache,
):
    particles, steps = tokens.shape
    _, kv, context, head_size = key_cache.shape
    local_heads = w_query.shape[1] // head_size
    vocab_rows, depth = embedding.shape
    count = particles * steps
    rows = local_heads // kv * steps
    vmem = pl.BlockSpec(memory_space=pltpu.VMEM)
    smem = pl.BlockSpec(memory_space=pltpu.SMEM)
    hbm = pl.BlockSpec(memory_space=pl.ANY)
    dma = pltpu.SemaphoreType.DMA

    ids = jnp.concatenate([tokens, ancestors[:, None]], axis=1)
    ids = jnp.pad(ids, ((0, 0), (0, 128 - ids.shape[1])))
    all_ids = pl.pallas_call(
        functools.partial(ids_kernel, n),
        out_shape=jax.ShapeDtypeStruct((n, particles, 128), jnp.int32),
        in_specs=[vmem],
        out_specs=vmem,
        scratch_shapes=[dma((n - 1,)), dma((n - 1,))],
        compiler_params=pltpu.CompilerParams(collective_id=0, has_side_effects=True),
    )(ids)

    tile = 16 if vocab_rows % 16 == 0 else 8
    owned = pl.pallas_call(
        functools.partial(rows_kernel, n, particles, steps, tile),
        out_shape=jax.ShapeDtypeStruct((n * count, depth), jnp.bfloat16),
        in_specs=[smem, hbm],
        out_specs=vmem,
        scratch_shapes=[
            pltpu.VMEM((n * count, tile, depth), jnp.bfloat16),
            pltpu.VMEM((n * count, depth), jnp.float32),
            pltpu.SMEM((2, n * count + 1), jnp.int32),
            dma,
        ],
        compiler_params=pltpu.CompilerParams(vmem_limit_bytes=VMEM_LIMIT),
    )(all_ids, embedding)

    deltas = [d for r in range(1, n) for d in (r, -r)]
    widths = {r: particles for r in range(1, n)}
    slots = len(deltas)
    chips = heads // 2
    cosine, sine = tables(steps, head_size, context)
    bf16, f32 = jnp.bfloat16, jnp.float32
    return pl.pallas_call(
        functools.partial(main_kernel, n, heads, deltas, widths),
        out_shape=jax.ShapeDtypeStruct((particles, steps, local_heads * head_size), bf16),
        in_specs=[smem] + [vmem] * 4 + [hbm] * 5,
        out_specs=vmem,
        scratch_shapes=[
            pltpu.VMEM(w_query.shape, bf16),
            pltpu.VMEM(w_key.shape, bf16),
            pltpu.VMEM(w_value.shape, bf16),
            pltpu.VMEM(key_cache.shape, bf16),
            pltpu.VMEM(value_cache.shape, bf16),
            pltpu.VMEM((n - 1, count, depth), bf16),
            pltpu.VMEM((heads, count, depth), bf16),
            pltpu.VMEM((count, (local_heads + 2 * kv) * head_size), f32),
            pltpu.VMEM((particles, kv, rows, head_size), bf16),
            pltpu.VMEM((kv, count, head_size), bf16),
            pltpu.VMEM((kv, count, head_size), bf16),
            pltpu.VMEM((slots, particles, kv, rows, head_size), bf16),
            pltpu.VMEM((slots + 1, particles, kv, rows, head_size), bf16),
            pltpu.VMEM((slots + 1, rows, 128), f32),
            pltpu.VMEM((slots + 1, particles, kv, rows, head_size), bf16),
            pltpu.VMEM((slots + 1, rows, 128), f32),
            pltpu.VMEM((kv, particles * rows, head_size), f32),
            dma((5,)),
            dma((n - 1,)),
            dma((n - 1,)),
            dma((max(chips - 1, 1),)),
            dma((max(chips - 1, 1),)),
            dma((chips,)),
            dma((chips,)),
            dma((slots,)),
            dma((slots,)),
            dma((slots,)),
            dma((slots,)),
            dma((slots,)),
            dma((slots,)),
        ],
        compiler_params=pltpu.CompilerParams(
            collective_id=1, has_side_effects=True, vmem_limit_bytes=VMEM_LIMIT
        ),
    )(
        all_ids,
        owned,
        norm_gain.reshape(1, -1),
        jnp.asarray(cosine),
        jnp.asarray(sine),
        w_query,
        w_key,
        w_value,
        key_cache,
        value_cache,
    )


def solution(mesh):
    in_specs = (
        P(("groups", "particle"), None),
        P(("groups", "particle")),
        P("particle", "head"),
        P(),
        P(None, "head"),
        P(None, "head"),
        P(None, "head"),
        P(("groups", "particle"), "head", None, None),
        P(("groups", "particle"), "head", None, None),
    )
    out_specs = P(("groups", "particle"), None, "head")
    return jax.shard_map(
        functools.partial(per_device, mesh.shape["particle"], mesh.shape["head"]),
        mesh=mesh,
        in_specs=in_specs,
        out_specs=out_specs,
        check_vma=False,
    )
```

time: 146 us -> 73 us (0.50)
  blocking collectives: 76.3 us -> 0 us
  Pallas kernels: 0 us -> 68 us
  matrix products: 42.2 us -> 0 us
  between operations: 15 us -> 0.09 us
  waiting for transfers between devices: 6.58 us -> 0 us
  other arithmetic: 3.46 us -> 0.76 us
    pallas_call x0 -> x3, Pallas kernels: none -> 68 us  [the longest x1 52.7 us: per_device(): pl.pallas_call(functools.partial(main_kernel, n, heads, deltas, widths),...]
    dot_general x9 -> x0, matrix products: 42.2 us -> none  [the longest x1 15.3 us: per_device(): jnp.dot(one_hot, embedding, preferred_element_type=jnp.float32)]
    all_gather x3 -> x0, blocking collectives: 38.6 us -> none  [the longest x1 16.3 us: per_device(): every_query = lax.all_gather(queries, 'particle', axis=0, tiled=True)]
    unnamed x2 -> x0, blocking collectives: 37.8 us -> none
    reduce_scatter x2 -> x0, waiting for transfers between devices: 6.54 us -> none  [the longest x1 6.52 us: per_device(): lax.psum_scatter(jnp.dot(one_hot, embedding, preferred_element_type=jnp.f...]
    reduce_sum x3 -> x0, other arithmetic: 2.8 us -> none  [the longest x1 2.47 us: per_device(): totals = jnp.sum(weights, axis=-1)]
  transfers between devices with their start and end apart: 2 -> 0, of which waited for: 1 -> 0; matrix products, arithmetic and copies ran while one was open for 9% -> 0% of each run, Pallas kernels for 0% -> 0%
where the time goes in v1:
time: 73 us; the launch traced here: 72.2 us
  Pallas kernels  68 us (93%)
  local copies, waits for them, and re-layouts  3.43 us (5%)
  other arithmetic  0.76 us (1%)
    pallas_call x1, Pallas kernels, per_device(): pl.pallas_call(functools.partial(main_kernel, n, heads, deltas, widths),...  52.7 us
    pallas_call x1, Pallas kernels, per_device(): pl.pallas_call(functools.partial(ids_kernel, n), out_shape=jax.ShapeDtype...  8.57 us
    pallas_call x1, Pallas kernels, per_device(): pl.pallas_call(functools.partial(rows_kernel, n, particles, steps, tile),...  6.67 us

profile of v1, /device:TPU:0, one launch (start us, length us, event | category | flops | bytes accessed | tf_op | source)
XLA Modules:
  0.0 72.2 jit_solution(6098213344147620749)
XLA Ops:
  0.0 0.7 %copy.12 = s32[8,1]{1,0:T(8,128)S(1)} copy(s32[8,1]{0,1:T(1,128)} %bitcast.1) | data formatting | bytes 64 | tf_op jit(solution)/shard_map/broadcast_in_dim | solution.py:450
  0.7 0.8 %pad_add_fusion = s32[8,9]{1,0:T(8,128)S(1)} fusion(s32[8,1]{1,0:T(8,128)S(1)} %copy.12, s32[8,8]{1,0:T(8,128)} %param.11), kind=kLoop, calls=%fused_computation | loop fusion | flops 72 | bytes 576 | tf_op jit(solution)/shard_map/concatenate | solution.py:450
  1.5 0.6 pad.4.ids_ref
  2.1 8.6 %shard_map.109.ids_ref = s32[4,8,128]{2,1,0:T(8,128)} custom-call(s32[8,128]{1,0:T(8,128)} %pad.4.ids_ref), custom_call_target="tpu_custom_call" | custom-call | tf_op jit(solution)/shard_map/pallas_call | solution.py:452
  10.7 0.7 reshape.3.gain_ref
  11.4 0.0 copy-start.3
  11.4 0.7 copy-done.3
  12.1 0.0 copy-start
  12.1 0.0 copy-start.1
  12.1 0.0 copy-start.2
  12.1 0.0 copy-start.4
  12.1 0.0 copy-start.5
  12.1 6.7 %shard_map.110.rows_ref = bf16[256,1024]{1,0:T(8,128)(2,1)S(1)} custom-call(s32[4,8,128]{2,1,0:T(8,128)S(1)} %copy-done.3, bf16[16032,1024]{1,0:T(8,128)(2,1)} %table_ref.1), custom_call_target="tpu_custom_call" | custom-call | tf_op jit(solution)/shard_map/pallas_call | solution.py:462
  18.8 0.0 copy-done
  18.8 0.0 copy-done.1
  18.8 0.0 copy-done.2
  18.8 0.0 copy-done.4
  18.8 0.0 copy-done.5
  18.9 52.7 %shard_map.111 = bf16[8,8,1024]{2,1,0:T(8,128)(2,1)S(1)} custom-call(s32[4,8,128]{2,1,0:T(8,128)S(1)} %copy-done.3, bf16[256,1024]{1,0:T(8,128)(2,1)S(1)} %shard_map.110.rows_ref, bf16[1,4096]{1,0:T(2,128)(2,1)S(1)} %reshape.3.gain_ref, f32[8,128]{1,0:T(8,128)S(1)} %copy-done.5, f32[8,128]{1,0:T(8,128)S(1)} %copy-done.4, bf16[4096,1024]{1,0:T(8,128)(2,1)} %wq_hbm.1, ...), custom_call_target="tpu_custom_call" | custom-call | tf_op jit(solution)/shard_map/pallas_call | solution.py:482
  71.6 0.7 copy.14
Async XLA Ops:
  11.4 0.7 copy-start.3
  12.1 6.7 %copy-start = (bf16[4096,256]{1,0:T(8,128)(2,1)S(1)}, bf16[4096,256]{1,0:T(8,128)(2,1)}, u32[]{:S(2)}) copy-start(bf16[4096,256]{1,0:T(8,128)(2,1)} %wk_hbm.1) | copy-start | bytes 6291460
  12.1 6.7 %copy-start.1 = (bf16[8,2,256,128]{3,2,1,0:T(8,128)(2,1)S(1)}, bf16[8,2,256,128]{3,2,1,0:T(8,128)(2,1)}, u32[]{:S(2)}) copy-start(bf16[8,2,256,128]{3,2,1,0:T(8,128)(2,1)} %kc_hbm.1) | copy-start | bytes 3145732
  12.1 6.7 %copy-start.2 = (bf16[8,2,256,128]{3,2,1,0:T(8,128)(2,1)S(1)}, bf16[8,2,256,128]{3,2,1,0:T(8,128)(2,1)}, u32[]{:S(2)}) copy-start(bf16[8,2,256,128]{3,2,1,0:T(8,128)(2,1)} %vc_hbm.1) | copy-start | bytes 3145732
  12.1 6.7 %copy-start.4 = (f32[8,128]{1,0:T(8,128)S(1)}, f32[8,128]{1,0:T(8,128)}, u32[]{:S(2)}) copy-start(f32[8,128]{1,0:T(8,128)} %constant.7.clone.sin_ref) | copy-start | bytes 12292
  12.1 6.7 %copy-start.5 = (f32[8,128]{1,0:T(8,128)S(1)}, f32[8,128]{1,0:T(8,128)}, u32[]{:S(2)}) copy-start(f32[8,128]{1,0:T(8,128)} %constant.6.clone.cos_ref) | copy-start | bytes 12292
